TPU v7x, 128 devices: a whole 4x4x4 slice. The times are simulated.
128 devices in a mesh: dp: 64 (over z, x, y), col: 2 (over core).
Axes of the slice: x: 4, y: 4, z: 4, core: 2. Of those that a mesh axis runs over, the one named last changes fastest.
Arguments:
- embeddings: bfloat16 [327680, 4096], P('dp', 'col'), may hold values from -500 to 500
- start_basis: bfloat16 [4096, 128], P('col'), may hold values from -1 to 1
Outputs:
- projected: float32 [4096, 128], P('col')
- image_factor: float32 [128, 128], replicated
All inputs are finite; a program needn't handle non-finite values.
Results may differ from a plain program's by a relative error of at most 0.0014.
Values may be sent and summed in bfloat16 or wider, within the bound.
A program may use at most 128 MiB of HBM per device.

v0:
```python
import jax
import jax.numpy as jnp
from jax import lax
from jax.sharding import PartitionSpec as P


def gram_matrix(rows_in):
    return lax.dot_general(
        rows_in,
        rows_in,
        (((0,), (0,)), ((), ())),
        precision=lax.Precision.HIGHEST,
        preferred_element_type=jnp.float32,
    )


def whiten(rows_in, total):
    factor = jnp.linalg.cholesky(total)
    identity = jnp.eye(total.shape[0], dtype=total.dtype)
    inverse = lax.linalg.triangular_solve(factor, identity, left_side=True, lower=True)
    whitened = lax.dot_general(
        rows_in,
        inverse,
        (((1,), (1,)), ((), ())),
        precision=lax.Precision.HIGHEST,
        preferred_element_type=jnp.float32,
    )
    return (whitened, factor)


def on_device(embeddings, start_basis):
    rows_here = embeddings.shape[0]
    row_factor = (rows_here * lax.axis_size("dp")) ** (-0.5)
    partial_value = jnp.dot(embeddings, start_basis, preferred_element_type=jnp.float32)
    image_rows = lax.psum(partial_value, "col")
    first_gram = lax.psum(gram_matrix(image_rows), "dp")
    ortho_rows, first_factor = whiten(image_rows, first_gram)
    second_gram = lax.psum(gram_matrix(ortho_rows), "dp")
    final_rows, unused_factor = whiten(ortho_rows, second_gram)
    final_basis = final_rows.astype(jnp.bfloat16)
    image_factor = first_factor * row_factor
    local_terms = lax.dot_general(
        embeddings, final_basis, (((0,), (0,)), ((), ())), preferred_element_type=jnp.float32
    )
    return (lax.psum(local_terms, "dp") * row_factor, image_factor)


def solution(mesh):
    placed = (P("dp", "col"), P("col", None))
    return jax.shard_map(
        on_device, mesh=mesh, in_specs=placed, out_specs=(P("col", None), P()), check_vma=False
    )
```

profile of v0, /device:TPU:1, one launch (start us, length us, event | category | flops | bytes accessed | tf_op | source)
XLA Modules:
  0.0 509.0 jit_solution(4692596971757230266)
XLA Ops:
  7.2 0.0 all-reduce.5.cloned.1.call-start
  7.2 1.0 copy-done
  8.2 11.4 %fusion.11 = f32[5120,128]{1,0:T(8,128)} fusion(bf16[5120,2048]{1,0:T(8,128)(2,1)} %param.5, bf16[2048,128]{1,0:T(8,128)(2,1)S(1)} %copy-done), kind=kOutput, calls=%fused_computation.24 | convolution fusion | flops 2684354560 | bytes 24117248 | tf_op jit(solution)/shard_map/dot_general | solution.py:34
  19.6 0.0 all-reduce.5.cloned.1.call-update
  19.6 0.0 all-reduce.7.cloned.1.call-start
  19.7 31.5 %all-reduce.5.cloned.1.call-done = f32[5120,128]{1,0:T(8,128)} async-done(((f32[5120,128]{1,0:T(8,128)}), f32[5120,128]{1,0:T(8,128)}) %all-reduce.5.cloned.1.call-update) | async-done | bytes 2621456 | tf_op jit(solution)/shard_map/psum | solution.py:35
  51.2 7.4 %fusion.12 = f32[128,128]{0,1:T(8,128)} fusion(f32[5120,128]{1,0:T(8,128)} %all-reduce.5.cloned.1.call-done), kind=kOutput, calls=%fused_computation.25 | convolution fusion | flops 1006632960 | bytes 2686976 | tf_op jit(solution)/shard_map/dot_general | solution.py:8
  58.6 0.2 all-reduce.9.cloned.1.call-start
  58.9 120.8 %all-reduce.7.cloned.1.call-done = f32[128,128]{0,1:T(8,128)} async-done(((f32[128,128]{0,1:T(8,128)}), f32[128,128]{0,1:T(8,128)}) %all-reduce.7.cloned.1.call-update) | async-done | bytes 65552 | tf_op jit(solution)/shard_map/psum | solution.py:36
  179.6 0.9 copy.5
  180.6 0.9 fusion.8
  181.4 11.7 %cholesky.44 = f32[128,128]{1,0:T(8,128)S(1)} custom-call(f32[128,128]{1,0:T(8,128)S(1)} %fusion.8), custom_call_target="Cholesky" | custom-call | tf_op jit(solution)/shard_map/jit(cholesky)/cholesky | solution.py:18
  193.2 0.6 compare_reduce_fusion.1
  193.8 1.3 fusion.10
  195.1 9.8 %custom-call.6 = f32[1,128,128]{1,2,0:T(8,128)S(1)} custom-call(f32[1,128,128]{2,1,0:T(8,128)S(1)} %get-tuple-element.7), custom_call_target="InvertDiagBlocksLowerTriangular" | custom-call | tf_op jit(solution)/shard_map/triangular_solve/custom-call.0 | solution.py:20
  204.9 0.3 fusion.2
  205.2 3.9 fusion.13
  209.2 5.1 %fusion.14 = f32[128,128]{0,1:T(8,128)} fusion(f32[5120,128]{1,0:T(8,128)S(1)} %fusion.13), kind=kOutput, calls=%fused_computation.27 | convolution fusion | flops 1006632960 | bytes 2686976 | tf_op jit(solution)/shard_map/dot_general | solution.py:8
  214.3 0.0 all-reduce.11.cloned.1.call-start
  214.4 119.8 %all-reduce.9.cloned.1.call-done = f32[128,128]{0,1:T(8,128)} async-done(((f32[128,128]{0,1:T(8,128)}), f32[128,128]{0,1:T(8,128)}) %all-reduce.9.cloned.1.call-update) | async-done | bytes 65552 | tf_op jit(solution)/shard_map/psum | solution.py:38
  334.1 0.9 copy.7
  335.0 0.9 fusion.6
  335.9 11.7 %cholesky.55 = f32[128,128]{1,0:T(8,128)S(1)} custom-call(f32[128,128]{1,0:T(8,128)S(1)} %fusion.6), custom_call_target="Cholesky" | custom-call | tf_op jit(solution)/shard_map/jit(cholesky)/cholesky | solution.py:18
  347.7 0.6 compare_reduce_fusion
  348.3 0.7 fusion.4
  349.0 9.8 %custom-call.7 = f32[1,128,128]{1,2,0:T(8,128)S(1)} custom-call(f32[1,128,128]{2,1,0:T(8,128)S(1)} %fusion.4), custom_call_target="InvertDiagBlocksLowerTriangular" | custom-call | tf_op jit(solution)/shard_map/triangular_solve/custom-call.0 | solution.py:20
  358.8 0.3 fusion
  359.1 2.2 convolution_convert_fusion
  361.3 10.8 %convolution_bitcast_fusion = f32[2048,128]{0,1:T(8,128)} fusion(bf16[5120,128]{1,0:T(8,128)(2,1)S(1)} %convolution_convert_fusion, bf16[5120,2048]{1,0:T(8,128)(2,1)} %param.5), kind=kOutput, calls=%fused_computation.1 | convolution fusion | flops 2684354560 | bytes 23330816 | tf_op jit(solution)/shard_map/dot_general | solution.py:42
  372.1 127.7 %all-reduce.11.cloned.1.call-done = f32[2048,128]{0,1:T(8,128)} async-done(((f32[2048,128]{0,1:T(8,128)}), f32[2048,128]{0,1:T(8,128)}) %all-reduce.11.cloned.1.call-update) | async-done | bytes 1048592 | tf_op jit(solution)/shard_map/psum | solution.py:45
  499.8 1.3 broadcast_multiply_fusion
  501.2 1.3 copy.8
  (6 shorter events, 0.1 us)
Async XLA Ops:
  7.2 1.0 copy-start
  7.2 44.0 %all-reduce.5.cloned.1.call-start = ((), (), s32[]{:S(2)}) async-start(), calls=%async_computation | async-start | bytes 5242880 | tf_op jit(solution)/shard_map/psum | solution.py:35
  19.6 160.0 %all-reduce.7.cloned.1.call-start = ((), (), s32[]{:S(2)}) async-start(), calls=%async_computation.1 | async-start | bytes 131072 | tf_op jit(solution)/shard_map/psum | solution.py:36
  58.6 275.5 %all-reduce.9.cloned.1.call-start = ((), (), s32[]{:S(2)}) async-start(), calls=%async_computation.2 | async-start | bytes 131072 | tf_op jit(solution)/shard_map/psum | solution.py:38
  214.3 285.5 %all-reduce.11.cloned.1.call-start = ((), (), s32[]{:S(2)}) async-start(), calls=%async_computation.3 | async-start | bytes 2097152 | tf_op jit(solution)/shard_map/psum | solution.py:45
Sparse Core Ops, SparseCore 0:
  19.7 31.3 all-reduce.4
  58.7 120.8 all-reduce.6
  214.4 119.6 all-reduce.8
  372.3 127.5 all-reduce.10
where the time goes:
time: 511 us; the launch traced here: 509 us
  waiting for transfers between devices  400 us (78%)
  other arithmetic  49.4 us (10%)
  matrix products  41.5 us (8%)
  between operations  13.9 us (3%)
    psum x1, waiting for transfers between devices, on_device(): return (lax.psum(local_terms, 'dp') * row_factor, image_factor)  128 us
    psum x1, waiting for transfers between devices, on_device(): first_gram = lax.psum(gram_matrix(image_rows), 'dp')  121 us
    psum x1, waiting for transfers between devices, on_device(): second_gram = lax.psum(gram_matrix(ortho_rows), 'dp')  120 us
    psum x1, waiting for transfers between devices, on_device(): image_rows = lax.psum(partial_value, 'col')  31.5 us
    another operation x6, other arithmetic, whiten(): factor = jnp.linalg.cholesky(total)  24.8 us
    another operation x3, other arithmetic, whiten(): lax.linalg.triangular_solve(factor, identity, left_side=True, lower=True)  20.3 us
    dot_general x2, matrix products, gram_matrix(): lax.dot_general(rows_in, rows_in, (((0,), (0,)), ((), ())), precision=lax...  12.6 us
    dot_general x1, matrix products, on_device(): jnp.dot(embeddings, start_basis, preferred_element_type=jnp.float32)  11.4 us
  transfers between devices with their start and end apart: 4, of which 4 were waited for; matrix products, arithmetic and copies ran while one was open for 0% of the time, Pallas kernels for 0%

commit v1 on v0

v1 whole, which is shorter than its diff:
```python
import functools

import jax
import jax.numpy as jnp
from jax import lax
from jax.experimental import pallas as pl
from jax.experimental.pallas import tpu as pltpu
from jax.sharding import PartitionSpec as P

F32 = jnp.float32
BF16 = jnp.bfloat16
MESH = pl.DeviceIdType.MESH
CHUNK = 512
BLOCK = 512
LAG = 2


def stride_of(dim):
    return 1 + 3 * dim + 9 * ((dim * (dim - 1)) // 2)


def reduce_kernel(
    a_hbm, q_hbm, t_ref, qf_ref,
    a_v, p_own, p_other, img, t_own, r1, r2, r3, acc1, acc2,
    load_sem, q_sem, ps_sem, pr_sem, s_sem, r_sem, hs_sem, hr_sem, qs_sem, qr_sem,
):
    rows, cols = a_v.shape
    n_chunk = rows // CHUNK
    n_block = cols // BLOCK
    dp = lax.axis_index("dp")
    core = lax.axis_index("col")

    def load(i):
        sl = pl.ds(pl.multiple_of(i * CHUNK, CHUNK), CHUNK)
        return pltpu.make_async_copy(a_hbm.at[sl], a_v.at[sl], load_sem.at[i])

    q_copy = pltpu.make_async_copy(q_hbm, qf_ref.at[core], q_sem)
    q_copy.start()
    for i in range(n_chunk):
        load(i).start()

    sibling = {"dp": dp, "col": 1 - core}

    def peer(dim, offset):
        stride = stride_of(dim)
        me = (dp // stride) % 4
        to = (me + offset) % 4
        return to, {"dp": dp + (to - me) * stride, "col": core}

    barrier = pltpu.get_barrier_semaphore()
    pl.semaphore_signal(barrier, inc=1, device_id=sibling, device_id_type=MESH)
    for dim in range(3):
        for offset in range(1, 4):
            pl.semaphore_signal(
                barrier, inc=1, device_id=peer(dim, offset)[1], device_id_type=MESH
            )
    pl.semaphore_wait(barrier, 10)

    q_copy.wait()
    q_send = pltpu.make_async_remote_copy(
        src_ref=qf_ref.at[core], dst_ref=qf_ref.at[core], send_sem=qs_sem, recv_sem=qr_sem,
        device_id=sibling, device_id_type=MESH,
    )
    q_send.start()

    def p_copy(i):
        sl = pl.ds(pl.multiple_of(i * CHUNK, CHUNK), CHUNK)
        return pltpu.make_async_remote_copy(
            src_ref=p_own.at[sl], dst_ref=p_other.at[sl],
            send_sem=ps_sem.at[i], recv_sem=pr_sem.at[i],
            device_id=sibling, device_id_type=MESH,
        )

    def multiply(i):
        sl = pl.ds(pl.multiple_of(i * CHUNK, CHUNK), CHUNK)
        p_own[sl] = jnp.dot(a_v[sl], qf_ref[core], preferred_element_type=F32)

    def combine(i):
        sl = pl.ds(pl.multiple_of(i * CHUNK, CHUNK), CHUNK)
        total = (p_own[sl] + p_other[sl]).T
        high = total.astype(BF16)
        img[0:128, sl] = high
        img[128:256, sl] = (total - high.astype(F32)).astype(BF16)

    for i in range(LAG):
        load(i).wait()
        multiply(i)
        p_copy(i).start()

    def step(i, carry):
        load(i).wait()
        p_copy(i - LAG).wait_recv()
        multiply(i)
        combine(i - LAG)
        p_copy(i).start()
        return carry

    lax.fori_loop(LAG, n_chunk, step, 0)
    for i in range(n_chunk - LAG, n_chunk):
        p_copy(i).wait_recv()
        combine(i)

    def dims(b):
        first = (2 * b + core) % 3
        return [(first + s) % 3 for s in range(3)]

    def position(dim):
        return (dp // stride_of(dim)) % 4

    def send(b, stage, offset):
        dim = dims(b)
        pos = [position(d) for d in dim]
        level = stage if stage < 3 else 5 - stage
        to, device = peer(dim[level], offset)
        c0 = b * BLOCK
        if stage == 0:
            src = t_own.at[pl.ds(pl.multiple_of(to * 32, 32), 32), pl.ds(c0, BLOCK)]
            dst = r1.at[b, offset - 1]
        elif stage == 1:
            src = acc1.at[b, pl.ds(pl.multiple_of(to * 8, 8), 8)]
            dst = r2.at[b, offset - 1]
        elif stage == 2:
            src = acc2.at[b, :, pl.ds(pl.multiple_of(to * 128, 128), 128)]
            dst = r3.at[b, offset - 1]
        else:
            if stage == 3:
                rsl = pl.ds(pl.multiple_of(pos[0] * 32 + pos[1] * 8, 8), 8)
                csl = pl.ds(pl.multiple_of(c0 + pos[2] * 128, 128), 128)
            elif stage == 4:
                rsl = pl.ds(pl.multiple_of(pos[0] * 32 + pos[1] * 8, 8), 8)
                csl = pl.ds(c0, BLOCK)
            else:
                rsl = pl.ds(pl.multiple_of(pos[0] * 32, 32), 32)
                csl = pl.ds(c0, BLOCK)
            src = t_ref.at[core, rsl, csl]
            dst = t_ref.at[core, rsl, csl]
        return pltpu.make_async_remote_copy(
            src_ref=src, dst_ref=dst,
            send_sem=s_sem.at[b, stage, offset - 1], recv_sem=r_sem.at[b, stage, offset - 1],
            device_id=device, device_id_type=MESH,
        )

    def half(b):
        piece = t_ref.at[core, :, pl.ds(b * BLOCK, BLOCK)]
        return pltpu.make_async_remote_copy(
            src_ref=piece, dst_ref=piece, send_sem=hs_sem.at[b], recv_sem=hr_sem.at[b],
            device_id=sibling, device_id_type=MESH,
        )

    def start(b, stage):
        for offset in range(1, 4):
            send(b, stage, offset).start()

    def receive(b, stage):
        for offset in range(1, 4):
            send(b, stage, offset).wait_recv()

    def advance(b, stage):
        dim = dims(b)
        pos = [position(d) for d in dim]
        c0 = b * BLOCK
        receive(b, stage)
        if stage == 0:
            own = t_own[pl.ds(pl.multiple_of(pos[0] * 32, 32), 32), pl.ds(c0, BLOCK)]
            acc1[b] = (own + r1[b, 0]) + (r1[b, 1] + r1[b, 2])
        elif stage == 1:
            own = acc1[b, pl.ds(pl.multiple_of(pos[1] * 8, 8), 8)]
            acc2[b] = (own + r2[b, 0]) + (r2[b, 1] + r2[b, 2])
        elif stage == 2:
            own = acc2[b, :, pl.ds(pl.multiple_of(pos[2] * 128, 128), 128)]
            rsl = pl.ds(pl.multiple_of(pos[0] * 32 + pos[1] * 8, 8), 8)
            csl = pl.ds(pl.multiple_of(c0 + pos[2] * 128, 128), 128)
            t_ref[core, rsl, csl] = (own + r3[b, 0]) + (r3[b, 1] + r3[b, 2])
        if stage < 5:
            start(b, stage + 1)
        else:
            half(b).start()

    for turn in range(n_block + 6):
        if turn < n_block:
            csl = pl.ds(turn * BLOCK, BLOCK)
            both = jnp.dot(img[...], a_v[:, csl], preferred_element_type=F32)
            t_own[:, csl] = both[0:128] + both[128:256]
            start(turn, 0)
        for b in range(n_block):
            stage = turn - 1 - b
            if 0 <= stage < 6:
                advance(b, stage)

    for b in range(n_block):
        half(b).wait_recv()
    q_send.wait()
    for i in range(n_chunk):
        p_copy(i).wait_send()
    for b in range(n_block):
        for stage in range(6):
            for offset in range(1, 4):
                send(b, stage, offset).wait_send()
        half(b).wait_send()


def split3(x):
    high = x.astype(BF16)
    rest = x - high.astype(F32)
    mid = rest.astype(BF16)
    low = (rest - mid.astype(F32)).astype(BF16)
    return jnp.concatenate([high, mid, low], 0)


def fold3(x):
    n = x.shape[0] // 3
    return x[0:n] + (x[n : 2 * n] + x[2 * n :])


def factor_and_inverse(gram, want_factor, step=8):
    n = gram.shape[0]
    gram = 0.5 * (gram + gram.T)
    lane = lax.broadcasted_iota(jnp.int32, (n, n), 1)
    row = lax.broadcasted_iota(jnp.int32, (n, n), 0)
    rest = gram
    inverse = []
    factor = None
    for c0 in range(0, n, step):
        m_rows = n - c0
        cols = [
            jnp.broadcast_to(rest[:, c0 + k : c0 + k + 1], (m_rows, n)) for k in range(step)
        ]
        ln = lane[c0:]
        rw = row[:m_rows]
        eye = jnp.where(ln == rw + c0, 1.0, 0.0).astype(F32)
        rest = jnp.where((ln >= c0) & (ln < c0 + step), eye, rest)
        scale = jnp.zeros((step, n), F32)
        part = jnp.zeros((m_rows, n), F32)
        for k in range(step):
            pivot = cols[k][k : k + 1]
            root = lax.rsqrt(pivot)
            scale = jnp.where(rw[:step] == k, root, scale)
            if want_factor:
                part = jnp.where((ln == c0 + k) & (rw >= k), cols[k] * root, part)
            mult = jnp.where(rw > k, cols[k] * (1.0 / pivot), 0.0)
            for later in range(k + 1, step):
                cols[later] = cols[later] - mult * cols[later][k : k + 1]
            rest = rest - mult * rest[k : k + 1]
        inverse.append(rest[:step] * scale)
        if want_factor:
            if c0:
                part = jnp.concatenate([factor[:c0], factor[c0:] + part], 0)
            factor = part
        rest = rest[step:]
    inverse = jnp.where(lane <= row, jnp.concatenate(inverse, 0), 0.0)
    return inverse, factor


def small_kernel(row_factor, t_ref, q_ref, out_ref, factor_ref, s_ref, w_ref):
    nt = (((1,), (1,)), ((), ()))
    core = lax.axis_index("col")
    gram = jnp.zeros((128, 128), F32)
    for c in range(2):
        gram += fold3(jnp.dot(split3(t_ref[c]), q_ref[c], preferred_element_type=F32))
    inverse, factor = factor_and_inverse(gram, True)
    factor_ref[...] = factor * row_factor
    gram = jnp.zeros((128, 128), F32)
    inverse3 = split3(inverse)
    for c in range(2):
        s_ref[c] = jnp.dot(
            inverse, t_ref[c], precision=lax.Precision.HIGHEST, preferred_element_type=F32
        )
        w_ref[...] = fold3(
            lax.dot_general(inverse3, q_ref[c], nt, preferred_element_type=F32)
        )
        gram += lax.dot_general(
            s_ref[c], w_ref[...], nt, precision=lax.Precision.HIGHEST, preferred_element_type=F32
        )
    inverse, _ = factor_and_inverse(gram, False)
    final = jnp.dot(
        inverse * row_factor, s_ref[core], precision=lax.Precision.HIGHEST,
        preferred_element_type=F32,
    )
    out_ref[...] = final.T


def on_device(embeddings, start_basis):
    rows, cols = embeddings.shape
    k = start_basis.shape[1]
    n_block = cols // BLOCK
    n_chunk = rows // CHUNK
    row_factor = (rows * lax.axis_size("dp")) ** (-0.5)
    vmem = pl.BlockSpec(memory_space=pltpu.VMEM)
    anywhere = pl.BlockSpec(memory_space=pl.ANY)
    dma = pltpu.SemaphoreType.DMA
    total, basis = pl.pallas_call(
        reduce_kernel,
        out_shape=[
            jax.ShapeDtypeStruct((2, k, cols), F32),
            jax.ShapeDtypeStruct((2, cols, k), BF16),
        ],
        in_specs=[anywhere, anywhere],
        out_specs=[vmem, vmem],
        scratch_shapes=[
            pltpu.VMEM((rows, cols), BF16),
            pltpu.VMEM((rows, k), F32),
            pltpu.VMEM((rows, k), F32),
            pltpu.VMEM((2 * k, rows), BF16),
            pltpu.VMEM((k, cols), F32),
            pltpu.VMEM((n_block, 3, 32, BLOCK), F32),
            pltpu.VMEM((n_block, 3, 8, BLOCK), F32),
            pltpu.VMEM((n_block, 3, 8, 128), F32),
            pltpu.VMEM((n_block, 32, BLOCK), F32),
            pltpu.VMEM((n_block, 8, BLOCK), F32),
            dma((n_chunk,)), dma, dma((n_chunk,)), dma((n_chunk,)),
            dma((n_block, 6, 3)), dma((n_block, 6, 3)),
            dma((n_block,)), dma((n_block,)), dma, dma,
        ],
        compiler_params=pltpu.CompilerParams(
            collective_id=0, has_side_effects=True, vmem_limit_bytes=48 * 2**20
        ),
        name="image_and_sum",
    )(embeddings, start_basis)
    return tuple(
        pl.pallas_call(
            functools.partial(small_kernel, row_factor),
            out_shape=[
                jax.ShapeDtypeStruct((cols, k), F32),
                jax.ShapeDtypeStruct((k, k), F32),
            ],
            in_specs=[vmem, vmem],
            out_specs=[vmem, vmem],
            scratch_shapes=[pltpu.VMEM((2, k, cols), F32), pltpu.VMEM((k, cols), F32)],
            compiler_params=pltpu.CompilerParams(vmem_limit_bytes=32 * 2**20),
            name="whiten",
        )(total, basis)
    )


def solution(mesh):
    placed = (P("dp", "col"), P("col", None))
    return jax.shard_map(
        on_device, mesh=mesh, in_specs=placed, out_specs=(P("col", None), P()), check_vma=False
    )
```

time: 511 us -> 87.8 us (0.17)
  waiting for transfers between devices: 400 us -> 0 us
  Pallas kernels: 0 us -> 86 us
  other arithmetic: 49.4 us -> 0 us
  matrix products: 41.5 us -> 0 us
  between operations: 13.9 us -> 0.65 us
    psum x4 -> x0, waiting for transfers between devices: 400 us -> none  [the longest x1 128 us: on_device(): return (lax.psum(local_terms, 'dp') * row_factor, image_factor)]
    pallas_call x0 -> x2, Pallas kernels: none -> 86 us  [the longest x1 67.2 us: on_device(): pl.pallas_call(reduce_kernel, out_shape=[jax.ShapeDtypeStruct((2, k, cols...]
    another operation x9 -> x0, other arithmetic: 45 us -> none  [the longest x6 24.8 us: whiten(): factor = jnp.linalg.cholesky(total)]
    dot_general x6 -> x0, matrix products: 40.9 us -> none  [the longest x2 12.6 us: gram_matrix(): lax.dot_general(rows_in, rows_in, (((0,), (0,)), ((), ())), precision=lax...]
  transfers between devices with their start and end apart: 4 -> 0, of which waited for: 4 -> 0; matrix products, arithmetic and copies ran while one was open for 0% -> 0% of each run, Pallas kernels for 0% -> 0%
where the time goes in v1:
time: 87.8 us; the launch traced here: 87.6 us
  Pallas kernels  86 us (98%)
  local copies, waits for them, and re-layouts  1.03 us (1%)
    pallas_call x1, Pallas kernels, on_device(): pl.pallas_call(reduce_kernel, out_shape=[jax.ShapeDtypeStruct((2, k, cols...  67.2 us
    pallas_call x1, Pallas kernels, on_device(): pl.pallas_call(functools.partial(small_kernel, row_factor), out_shape=[ja...  18.7 us

profile of v1, /device:TPU:1, one launch (start us, length us, event | category | flops | bytes accessed | tf_op | source)
XLA Modules:
  0.0 87.6 jit_solution(2152178909713489198)
XLA Ops:
  0.6 0.0 copy-start
  0.6 1.0 %copy-done = bf16[2048,128]{1,0:T(8,128)(2,1)S(1)} copy-done((bf16[2048,128]{1,0:T(8,128)(2,1)S(1)}, bf16[2048,128]{1,0:T(8,128)(2,1)}, u32[]{:S(2)}) %copy-start) | copy-done | bytes 524312
  1.7 67.2 %image_and_sum.1 = (f32[2,128,2048]{2,1,0:T(8,128)S(1)}, bf16[2,2048,128]{2,1,0:T(8,128)(2,1)S(1)}) custom-call(bf16[5120,2048]{1,0:T(8,128)(2,1)} %a_hbm.1, bf16[2048,128]{1,0:T(8,128)(2,1)S(1)} %copy-done), custom_call_target="tpu_custom_call" | custom-call | tf_op jit(solution)/shard_map/image_and_sum/pallas_call | solution.py:291
  68.9 18.7 %whiten.1 = (f32[2048,128]{1,0:T(8,128)}, f32[128,128]{1,0:T(8,128)}) custom-call(f32[2,128,2048]{2,1,0:T(8,128)S(1)} %get-tuple-element.4.t_ref, bf16[2,2048,128]{2,1,0:T(8,128)(2,1)S(1)} %get-tuple-element.5.q_ref), custom_call_target="tpu_custom_call" | custom-call | tf_op jit(solution)/shard_map/whiten/pallas_call | solution.py:320
Async XLA Ops:
  0.6 1.0 %copy-start = (bf16[2048,128]{1,0:T(8,128)(2,1)S(1)}, bf16[2048,128]{1,0:T(8,128)(2,1)}, u32[]{:S(2)}) copy-start(bf16[2048,128]{1,0:T(8,128)(2,1)} %q_hbm.1) | copy-start | bytes 1572868

commit v2 on v0

v2 whole, which is shorter than its diff:
```python
import functools

import jax
import jax.numpy as jnp
from jax import lax
from jax.experimental import pallas as pl
from jax.experimental.pallas import tpu as pltpu
from jax.sharding import PartitionSpec as P

F32 = jnp.float32
BF16 = jnp.bfloat16
MESH = pl.DeviceIdType.MESH
CHUNK = 512
BLOCK = 512
LAG = 3
FLIGHT = 3
WIDTH, STEP = 32, 8
ORDER = (
    ("T", 1), ("T", 2), ("T", 3), ("G", 0), ("A", 0), ("A", 1), ("A", 2), ("G", 1), ("A", 3), ("B", 0),
    ("B", 1), ("G", 2), ("B", 2), ("H", 0), ("B", 3), ("E", 0), ("C", 0), ("C", 1), ("E", 1), ("C", 2),
    ("E", 2), ("C", 3), ("E", 3), ("W", 0), ("D", 0), ("S", 0), ("D", 1), ("S", 1), ("D", 2), ("S", 2),
    ("D", 3), ("S", 3),
)


STRIDES = (1, 4, 16)


def reduce_kernel(
    a_hbm, q_hbm, s_ref, gram_ref, factor_ref,
    a_v, q_v, p_own, p_other, img, t_own, t_sum, r1, r2, acc1,
    g_in, g_src, g_full, inv_v, fac_v, w_v, g2,
    load_sem, q_sem, ps_sem, pr_sem, s_sem, r_sem, gs_sem, gr_sem, hs_sem, hr_sem,
):
    rows, cols = a_v.shape
    n_chunk = rows // CHUNK
    n_block = cols // BLOCK
    dp = lax.axis_index("dp")
    core = lax.axis_index("col")

    def load(i):
        sl = pl.ds(pl.multiple_of(i * CHUNK, CHUNK), CHUNK)
        return pltpu.make_async_copy(a_hbm.at[sl], a_v.at[sl], load_sem.at[i])

    q_copy = pltpu.make_async_copy(q_hbm, q_v, q_sem)
    q_copy.start()
    for i in range(FLIGHT):
        load(i).start()

    sibling = {"dp": dp, "col": 1 - core}

    place = [lax.rem(lax.div(dp, stride), 4) for stride in STRIDES]
    onward = [[lax.rem(place[d] + offset, 4) for offset in range(4)] for d in range(3)]
    delta = [[(to - place[d]) * STRIDES[d] for to in onward[d]] for d in range(3)]

    def either(zero, one):
        return zero + core * (one - zero)

    orders = []
    for f in range(3):
        pair = [((f + s) % 3, (f + s + 1) % 3) for s in range(3)]
        orders.append((
            [either(place[d], place[e]) for d, e in pair],
            [[either(onward[d][o], onward[e][o]) for o in range(4)] for d, e in pair],
            [[either(delta[d][o], delta[e][o]) for o in range(4)] for d, e in pair],
        ))

    def device(shift):
        return {"dp": dp + shift, "col": core}

    barrier = pltpu.get_barrier_semaphore()
    pl.semaphore_signal(barrier, inc=1, device_id=sibling, device_id_type=MESH)
    shifts = [delta[d][o] for d in range(3) for o in range(1, 4)]
    shifts += [
        delta[d][o] + delta[(d + 1) % 3][u]
        for d in range(3) for o in range(1, 4) for u in range(1, 4)
    ]
    for shift in shifts:
        pl.semaphore_signal(barrier, inc=1, device_id=device(shift), device_id_type=MESH)

    def p_copy(i):
        sl = pl.ds(pl.multiple_of(i * CHUNK, CHUNK), CHUNK)
        return pltpu.make_async_remote_copy(
            src_ref=p_own.at[sl], dst_ref=p_other.at[sl],
            send_sem=ps_sem.at[i], recv_sem=pr_sem.at[i],
            device_id=sibling, device_id_type=MESH,
        )

    def multiply(i):
        sl = pl.ds(pl.multiple_of(i * CHUNK, CHUNK), CHUNK)
        p_own[sl] = jnp.dot(a_v[sl], q_v[...], preferred_element_type=F32)

    def combine(i):
        sl = pl.ds(pl.multiple_of(i * CHUNK, CHUNK), CHUNK)
        total = (p_own[sl] + p_other[sl]).T
        high = total.astype(BF16)
        img[0:128, sl] = high
        img[128:256, sl] = (total - high.astype(F32)).astype(BF16)

    q_copy.wait()
    for i in range(LAG):
        load(i).wait()
        load(i + FLIGHT).start()
        multiply(i)
    pl.semaphore_wait(barrier, 1 + len(shifts))
    for i in range(LAG):
        p_copy(i).start()

    def step(i, carry):
        load(i).wait()

        @pl.when(i + FLIGHT < n_chunk)
        def _():
            load(i + FLIGHT).start()

        p_copy(i - LAG).wait_recv()
        multiply(i)
        combine(i - LAG)
        p_copy(i).start()
        return carry

    lax.fori_loop(LAG, n_chunk, step, 0)
    for i in range(n_chunk - LAG, n_chunk - 1):
        p_copy(i).wait_recv()
        combine(i)

    def gram_send(stage, offset):
        here, _, shift = orders[0]
        return pltpu.make_async_remote_copy(
            src_ref=g_src.at[stage], dst_ref=g_in.at[stage, here[stage]],
            send_sem=gs_sem.at[stage, offset - 1], recv_sem=gr_sem.at[stage, offset - 1],
            device_id=device(shift[stage][offset]), device_id_type=MESH,
        )

    def gram_start(stage, value):
        g_src[stage] = value
        g_in[stage, orders[0][0][stage]] = value
        for offset in range(1, 4):
            gram_send(stage, offset).start()

    def gram_half():
        return pltpu.make_async_remote_copy(
            src_ref=g_full.at[core], dst_ref=g_full.at[core],
            send_sem=hs_sem.at[0], recv_sem=hr_sem.at[0],
            device_id=sibling, device_id_type=MESH,
        )

    def gram_advance(stage):
        for offset in range(1, 4):
            gram_send(stage, offset).wait_recv()
        value = (g_in[stage, 0] + g_in[stage, 1]) + (g_in[stage, 2] + g_in[stage, 3])
        if stage < 2:
            gram_start(stage + 1, value)
        else:
            g_full[core] = value
            gram_half().start()

    nt = (((1,), (1,)), ((), ()))
    early = rows - CHUNK

    def quad(rsl):
        part = img[:, rsl]
        both = lax.dot_general(part, part, nt, preferred_element_type=F32)
        return (both[0:128, 0:128] + both[128:256, 128:256]) + (
            both[0:128, 128:256] + both[128:256, 0:128]
        )

    def block(rsl, csl):
        both = jnp.dot(img[:, rsl], a_v[rsl, csl], preferred_element_type=F32)
        return both[0:128] + both[128:256]

    def send(b, stage, offset):
        here, there, shift = orders[2 * b % 3]
        c0 = b * BLOCK
        if stage in (0, 3):
            move = shift[0][offset]
            slot = 11 * stage + offset - 1
        else:
            o1, o2 = divmod(offset, 4)
            move = shift[1][o1] + shift[2][o2]
            slot = 3 + (stage - 1) * 15 + offset - 1
        if stage == 0:
            src = t_own.at[pl.ds(pl.multiple_of(there[0][offset] * 32, 32), 32), pl.ds(c0, BLOCK)]
            dst = r1.at[b, offset - 1]
        elif stage == 1:
            rsl = pl.ds(pl.multiple_of(there[1][o1] * 8, 8), 8)
            csl = pl.ds(pl.multiple_of(there[2][o2] * 128, 128), 128)
            src = acc1.at[b, rsl, csl]
            dst = r2.at[b, offset - 1]
        else:
            if stage == 2:
                rsl = pl.ds(pl.multiple_of(here[0] * 32 + here[1] * 8, 8), 8)
                csl = pl.ds(pl.multiple_of(c0 + here[2] * 128, 128), 128)
            else:
                rsl = pl.ds(pl.multiple_of(here[0] * 32, 32), 32)
                csl = pl.ds(c0, BLOCK)
            src = t_sum.at[rsl, csl]
            dst = t_sum.at[rsl, csl]
        return pltpu.make_async_remote_copy(
            src_ref=src, dst_ref=dst, send_sem=s_sem.at[b, slot], recv_sem=r_sem.at[b, slot],
            device_id=device(move), device_id_type=MESH,
        )

    def offsets(stage):
        return range(1, 4) if stage in (0, 3) else range(1, 16)

    def start(b, stage):
        for offset in offsets(stage):
            send(b, stage, offset).start()

    def advance(b, stage):
        here = orders[2 * b % 3][0]
        c0 = b * BLOCK
        for offset in offsets(stage):
            send(b, stage, offset).wait_recv()
        if stage == 0:
            own = t_own[pl.ds(pl.multiple_of(here[0] * 32, 32), 32), pl.ds(c0, BLOCK)]
            acc1[b] = (own + r1[b, 0]) + (r1[b, 1] + r1[b, 2])
        elif stage == 1:
            rsl = pl.ds(pl.multiple_of(here[1] * 8, 8), 8)
            csl = pl.ds(pl.multiple_of(here[2] * 128, 128), 128)
            parts = [acc1[b, rsl, csl]] + [r2[b, i] for i in range(15)]
            while len(parts) > 1:
                parts = [parts[i] + parts[i + 1] for i in range(0, len(parts), 2)]
            rsl = pl.ds(pl.multiple_of(here[0] * 32 + here[1] * 8, 8), 8)
            csl = pl.ds(pl.multiple_of(c0 + here[2] * 128, 128), 128)
            t_sum[rsl, csl] = parts[0]
        if stage < 3:
            start(b, stage + 1)

    t_own[:, 0:BLOCK] = block(pl.ds(0, early), pl.ds(0, BLOCK))
    inv_v[...] = quad(pl.ds(0, early))
    p_copy(n_chunk - 1).wait_recv()
    combine(n_chunk - 1)
    t_own[:, 0:BLOCK] += block(pl.ds(early, CHUNK), pl.ds(0, BLOCK))
    start(0, 0)
    inv_v[...] += quad(pl.ds(early, CHUNK))
    gram_start(0, inv_v[pl.ds(pl.multiple_of(core * 64, 64), 64)])

    for kind, n in ORDER:
        if kind == "T":
            csl = pl.ds(n * BLOCK, BLOCK)
            t_own[:, csl] = block(pl.ds(0, rows), csl)
            start(n, 0)
        elif kind == "G":
            gram_advance(n)
        elif kind == "H":
            gram_half().wait_recv()
            gram = g_full[...].reshape(128, 128)
            inv_v[...] = 0.5 * (gram + gram.T)
            fac_v[...] = jnp.zeros_like(fac_v)
        elif kind == "E":
            c0 = n * WIDTH
            done, rest, fac_v[c0:] = eliminate(inv_v[c0:], fac_v[c0:], c0, WIDTH, STEP)
            inv_v[c0 : c0 + WIDTH] = done
            if c0 + WIDTH < 128:
                inv_v[c0 + WIDTH :] = rest
        elif kind == "W":
            inv_v[...] = lower(inv_v[...])
            factor_ref[...] = fac_v[...]
            w_v[...] = fold3(
                lax.dot_general(split3(inv_v[...]), q_v[...], nt, preferred_element_type=F32)
            )
        elif kind == "S":
            csl = pl.ds(n * BLOCK, BLOCK)
            s_ref[:, csl] = jnp.dot(
                inv_v[...], t_sum[:, csl], precision=lax.Precision.HIGHEST,
                preferred_element_type=F32,
            )
            part = lax.dot_general(
                s_ref[:, csl], w_v[:, csl], nt, precision=lax.Precision.HIGHEST,
                preferred_element_type=F32,
            )
            g2[core] = part if n == 0 else g2[core] + part
        else:
            advance(n, "ABCD".index(kind))

    g2_copy = pltpu.make_async_remote_copy(
        src_ref=g2.at[core], dst_ref=g2.at[core], send_sem=hs_sem.at[1], recv_sem=hr_sem.at[1],
        device_id=sibling, device_id_type=MESH,
    )
    g2_copy.start()
    for i in range(n_chunk):
        p_copy(i).wait_send()
    for b in range(n_block):
        for stage in range(4):
            for offset in offsets(stage):
                send(b, stage, offset).wait_send()
    for stage in range(3):
        for offset in range(1, 4):
            gram_send(stage, offset).wait_send()
    gram_half().wait_send()
    g2_copy.wait()
    gram_ref[...] = g2[0] + g2[1]


def eliminate(rest, factor, c0, width, step):
    size = rest.shape[1]
    done = []
    for start in range(c0, c0 + width, step):
        n = rest.shape[0]
        lane = lax.broadcasted_iota(jnp.int32, (n, size), 1)
        row = lax.broadcasted_iota(jnp.int32, (n, size), 0)
        cols = [jnp.broadcast_to(rest[:, start + k : start + k + 1], (n, size)) for k in range(step)]
        eye = jnp.where(lane == row + start, 1.0, 0.0).astype(F32)
        rest = jnp.where((lane >= start) & (lane < start + step), eye, rest)
        scale = jnp.zeros((step, size), F32)
        part = jnp.zeros((n, size), F32)
        for k in range(step):
            pivot = cols[k][k : k + 1]
            root = lax.rsqrt(pivot)
            scale = jnp.where(row[:step] == k, root, scale)
            if factor is not None:
                part = jnp.where((lane == start + k) & (row >= k), cols[k] * root, part)
            mult = jnp.where(row > k, cols[k] * (1.0 / pivot), 0.0)
            for later in range(k + 1, step):
                cols[later] = cols[later] - mult * cols[later][k : k + 1]
            rest = rest - mult * rest[k : k + 1]
        if factor is not None:
            ahead = factor.shape[0] - n
            factor = factor + part if not ahead else jnp.concatenate(
                [factor[:ahead], factor[ahead:] + part], 0
            )
        done.append(rest[:step] * scale)
        rest = rest[step:]
    return jnp.concatenate(done, 0), rest, factor


def split3(x):
    high = x.astype(BF16)
    rest = x - high.astype(F32)
    mid = rest.astype(BF16)
    low = (rest - mid.astype(F32)).astype(BF16)
    return jnp.concatenate([high, mid, low], 0)


def fold3(x):
    n = x.shape[0] // 3
    return x[0:n] + (x[n : 2 * n] + x[2 * n :])


def lower(x):
    lane = lax.broadcasted_iota(jnp.int32, x.shape, 1)
    row = lax.broadcasted_iota(jnp.int32, x.shape, 0)
    return jnp.where(lane <= row, x, 0.0)


def final_kernel(row_factor, s_ref, gram_ref, factor_ref, out_ref, scaled_ref):
    scaled_ref[...] = factor_ref[...] * row_factor
    gram = gram_ref[...]
    inverse, _, _ = eliminate(0.5 * (gram + gram.T), None, 0, gram.shape[0], STEP)
    inverse = lower(inverse) * row_factor
    final = jnp.dot(
        inverse, s_ref[...], precision=lax.Precision.HIGHEST, preferred_element_type=F32
    )
    out_ref[...] = final.T


def on_device(embeddings, start_basis):
    rows, cols = embeddings.shape
    k = start_basis.shape[1]
    n_block = cols // BLOCK
    n_chunk = rows // CHUNK
    row_factor = (rows * lax.axis_size("dp")) ** (-0.5)
    vmem = pl.BlockSpec(memory_space=pltpu.VMEM)
    anywhere = pl.BlockSpec(memory_space=pltpu.HBM)
    dma = pltpu.SemaphoreType.DMA
    whitened, gram, factor = pl.pallas_call(
        reduce_kernel,
        out_shape=[
            jax.ShapeDtypeStruct((k, cols), F32),
            jax.ShapeDtypeStruct((k, k), F32),
            jax.ShapeDtypeStruct((k, k), F32),
        ],
        in_specs=[anywhere, anywhere],
        out_specs=[vmem, vmem, vmem],
        scratch_shapes=[
            pltpu.VMEM((rows, cols), BF16),
            pltpu.VMEM((cols, k), BF16),
            pltpu.VMEM((rows, k), F32),
            pltpu.VMEM((rows, k), F32),
            pltpu.VMEM((2 * k, rows), BF16),
            pltpu.VMEM((k, cols), F32),
            pltpu.VMEM((k, cols), F32),
            pltpu.VMEM((n_block, 3, 32, BLOCK), F32),
            pltpu.VMEM((n_block, 15, 8, 128), F32),
            pltpu.VMEM((n_block, 32, BLOCK), F32),
            pltpu.VMEM((3, 4, k // 2, k), F32),
            pltpu.VMEM((3, k // 2, k), F32),
            pltpu.VMEM((2, k // 2, k), F32),
            pltpu.VMEM((k, k), F32),
            pltpu.VMEM((k, k), F32),
            pltpu.VMEM((k, cols), F32),
            pltpu.VMEM((2, k, k), F32),
            dma((n_chunk,)), dma, dma((n_chunk,)), dma((n_chunk,)),
            dma((n_block, 36)), dma((n_block, 36)),
            dma((3, 3)), dma((3, 3)), dma((2,)), dma((2,)),
        ],
        compiler_params=pltpu.CompilerParams(
            collective_id=0, has_side_effects=True, vmem_limit_bytes=52 * 2**20
        ),
        name="image_and_sum",
    )(embeddings, start_basis)
    return tuple(
        pl.pallas_call(
            functools.partial(final_kernel, row_factor),
            out_shape=[
                jax.ShapeDtypeStruct((cols, k), F32),
                jax.ShapeDtypeStruct((k, k), F32),
            ],
            in_specs=[vmem, vmem, vmem],
            out_specs=[vmem, vmem],
            compiler_params=pltpu.CompilerParams(vmem_limit_bytes=32 * 2**20),
            name="final",
        )(whitened, gram, factor)
    )


def solution(mesh):
    placed = (P("dp", "col"), P("col", None))
    return jax.shard_map(
        on_device, mesh=mesh, in_specs=placed, out_specs=(P("col", None), P()), check_vma=False
    )
```

time: 511 us -> 60.2 us (0.12)
  waiting for transfers between devices: 400 us -> 0 us
  Pallas kernels: 0 us -> 58.3 us
  other arithmetic: 49.4 us -> 0 us
  matrix products: 41.5 us -> 0 us
  between operations: 13.9 us -> 0.65 us
    psum x4 -> x0, waiting for transfers between devices: 400 us -> none  [the longest x1 128 us: on_device(): return (lax.psum(local_terms, 'dp') * row_factor, image_factor)]
    pallas_call x0 -> x2, Pallas kernels: none -> 58.3 us  [the longest x1 52.2 us: on_device(): pl.pallas_call(reduce_kernel, out_shape=[jax.ShapeDtypeStruct((k, cols),...]
    another operation x9 -> x0, other arithmetic: 45 us -> none  [the longest x6 24.8 us: whiten(): factor = jnp.linalg.cholesky(total)]
    dot_general x6 -> x0, matrix products: 40.9 us -> none  [the longest x2 12.6 us: gram_matrix(): lax.dot_general(rows_in, rows_in, (((0,), (0,)), ((), ())), precision=lax...]
  transfers between devices with their start and end apart: 4 -> 0, of which waited for: 4 -> 0; matrix products, arithmetic and copies ran while one was open for 0% -> 0% of each run, Pallas kernels for 0% -> 0%
where the time goes in v2:
time: 60.2 us; the launch traced here: 60 us
  Pallas kernels  58.3 us (97%)
  local copies, waits for them, and re-layouts  1.03 us (2%)
  between operations  0.65 us (1%)
    pallas_call x1, Pallas kernels, on_device(): pl.pallas_call(reduce_kernel, out_shape=[jax.ShapeDtypeStruct((k, cols),...  52.2 us
    pallas_call x1, Pallas kernels, on_device(): pl.pallas_call(functools.partial(final_kernel, row_factor), out_shape=[ja...  6.1 us

profile of v2, /device:TPU:1, one launch (start us, length us, event | category | flops | bytes accessed | tf_op | source)
XLA Modules:
  0.0 60.0 jit_solution(6480443835555337961)
XLA Ops:
  0.6 0.0 copy-start
  0.6 1.0 %copy-done = bf16[2048,128]{1,0:T(8,128)(2,1)S(1)} copy-done((bf16[2048,128]{1,0:T(8,128)(2,1)S(1)}, bf16[2048,128]{1,0:T(8,128)(2,1)}, u32[]{:S(2)}) %copy-start) | copy-done | bytes 524312
  1.7 52.2 %image_and_sum.1 = (f32[128,2048]{1,0:T(8,128)S(1)}, f32[128,128]{1,0:T(8,128)S(1)}, f32[128,128]{1,0:T(8,128)S(1)}) custom-call(bf16[5120,2048]{1,0:T(8,128)(2,1)} %a_hbm.1, bf16[2048,128]{1,0:T(8,128)(2,1)S(1)} %copy-done), custom_call_target="tpu_custom_call" | custom-call | tf_op jit(solution)/shard_map/image_and_sum/pallas_call | solution.py:368
  53.9 6.1 %final.1 = (f32[2048,128]{1,0:T(8,128)}, f32[128,128]{1,0:T(8,128)}) custom-call(f32[128,2048]{1,0:T(8,128)S(1)} %get-tuple-element.5.s_ref, f32[128,128]{1,0:T(8,128)S(1)} %get-tuple-element.6.gram_ref, f32[128,128]{1,0:T(8,128)S(1)} %get-tuple-element.7.factor_ref), custom_call_target="tpu_custom_call" | custom-call | tf_op jit(solution)/shard_map/final/pallas_call | solution.py:405
Async XLA Ops:
  0.6 1.0 %copy-start = (bf16[2048,128]{1,0:T(8,128)(2,1)S(1)}, bf16[2048,128]{1,0:T(8,128)(2,1)}, u32[]{:S(2)}) copy-start(bf16[2048,128]{1,0:T(8,128)(2,1)} %q_hbm.1) | copy-start | bytes 1572868

commit v3 on v2

--- a/solution.py
+++ b/solution.py
@@ -15,12 +15,7 @@
 LAG = 3
 FLIGHT = 3
 WIDTH, STEP = 32, 8
-ORDER = (
-    ("T", 1), ("T", 2), ("T", 3), ("G", 0), ("A", 0), ("A", 1), ("A", 2), ("G", 1), ("A", 3), ("B", 0),
-    ("B", 1), ("G", 2), ("B", 2), ("H", 0), ("B", 3), ("E", 0), ("C", 0), ("C", 1), ("E", 1), ("C", 2),
-    ("E", 2), ("C", 3), ("E", 3), ("W", 0), ("D", 0), ("S", 0), ("D", 1), ("S", 1), ("D", 2), ("S", 2),
-    ("D", 3), ("S", 3),
-)
+ORDER = (("T", 1), ("T", 2), ("T", 3), ("G", 0), ("A", 0), ("A", 1), ("A", 2), ("G", 1), ("A", 3), ("B", 0), ("B", 1), ("G", 2), ("B", 2), ("H", 0), ("B", 3), ("E", 0), ("C", 0), ("C", 1), ("E", 1), ("C", 2), ("E", 2), ("C", 3), ("E", 3), ("W", 0), ("D", 0), ("S", 0), ("D", 1), ("S", 1), ("D", 2), ("S", 2), ("D", 3), ("S", 3), )
 
 
 STRIDES = (1, 4, 16)
@@ -44,8 +39,7 @@
 
     q_copy = pltpu.make_async_copy(q_hbm, q_v, q_sem)
     q_copy.start()
-    for i in range(FLIGHT):
-        load(i).start()
+    load(0).start()
 
     sibling = {"dp": dp, "col": 1 - core}
 
@@ -97,6 +91,8 @@
         img[0:128, sl] = high
         img[128:256, sl] = (total - high.astype(F32)).astype(BF16)
 
+    for i in range(1, FLIGHT):
+        load(i).start()
     q_copy.wait()
     for i in range(LAG):
         load(i).wait()
@@ -326,17 +322,58 @@
     return jnp.concatenate(done, 0), rest, factor
 
 
-def split3(x):
+def terms3(x):
     high = x.astype(BF16)
     rest = x - high.astype(F32)
     mid = rest.astype(BF16)
-    low = (rest - mid.astype(F32)).astype(BF16)
-    return jnp.concatenate([high, mid, low], 0)
+    return high, mid, (rest - mid.astype(F32)).astype(BF16)
+
+
+def split3(x):
+    return jnp.concatenate(terms3(x), 0)
 
 
 def fold3(x):
     n = x.shape[0] // 3
     return x[0:n] + (x[n : 2 * n] + x[2 * n :])
+
+
+def inverse_by_blocks(rest, step):
+    size = rest.shape[0]
+    lane = lax.broadcasted_iota(jnp.int32, (size, size), 1)
+    row = lax.broadcasted_iota(jnp.int32, (step, size), 0)
+    done = []
+    for start in range(0, size, step):
+        n = size - start
+        block = (lane >= start) & (lane < start + step)
+
+        def column(k, rows):
+            return jnp.broadcast_to(rows[:, start + k : start + k + 1], rows.shape)
+
+        cols = [column(k, rest[:step]) for k in range(step)]
+        eye = jnp.where(lane[:step] == row + start, 1.0, 0.0).astype(F32)
+        down = jnp.where(block[:step], eye, rest[:step])
+        full = down
+        pivots = []
+        for k in range(step):
+            pivots.append(cols[k][k : k + 1])
+            mult = cols[k] * (1.0 / pivots[k])
+            below = jnp.where(row > k, mult, 0.0)
+            others = jnp.where(row != k, mult, 0.0)
+            for later in range(k + 1, step):
+                cols[later] = cols[later] - others * cols[later][k : k + 1]
+            line = down[k : k + 1]
+            down = down - below * line
+            full = full - others * line
+        pivots = jnp.concatenate(pivots, 0)
+        done.append(down * lax.rsqrt(pivots))
+        if n > step:
+            full = full * (1.0 / pivots)
+            terms = [column(k, rest[step:]) * full[k : k + 1] for k in range(step)]
+            while len(terms) > 1:
+                terms = [terms[i] + terms[i + 1] for i in range(0, len(terms), 2)]
+            rest = jnp.where(block[: n - step], 0.0, rest[step:]) - terms[0]
+    return lower(jnp.concatenate(done, 0))
 
 
 def lower(x):
@@ -345,15 +382,16 @@
     return jnp.where(lane <= row, x, 0.0)
 
 
-def final_kernel(row_factor, s_ref, gram_ref, factor_ref, out_ref, scaled_ref):
+def final_kernel(row_factor, s_ref, gram_ref, factor_ref, out_ref, scaled_ref, right_v):
     scaled_ref[...] = factor_ref[...] * row_factor
+    high, mid, low = terms3(s_ref[...])
+    for place, term in enumerate((high, mid, high, mid, low, high)):
+        right_v[128 * place : 128 * (place + 1)] = term
     gram = gram_ref[...]
-    inverse, _, _ = eliminate(0.5 * (gram + gram.T), None, 0, gram.shape[0], STEP)
-    inverse = lower(inverse) * row_factor
-    final = jnp.dot(
-        inverse, s_ref[...], precision=lax.Precision.HIGHEST, preferred_element_type=F32
-    )
-    out_ref[...] = final.T
+    inverse = inverse_by_blocks(0.5 * (gram + gram.T), 2 * STEP) * row_factor
+    high, mid, low = terms3(inverse)
+    left = jnp.concatenate([high, high, mid, mid, high, low], 1)
+    out_ref[...] = jnp.dot(left, right_v[...], preferred_element_type=F32).T
 
 
 def on_device(embeddings, start_basis):
@@ -400,7 +438,7 @@
             collective_id=0, has_side_effects=True, vmem_limit_bytes=52 * 2**20
         ),
         name="image_and_sum",
-    )(embeddings, start_basis)
+    )(embeddings, pltpu.with_memory_space_constraint(start_basis, pltpu.HBM))
     return tuple(
         pl.pallas_call(
             functools.partial(final_kernel, row_factor),
@@ -410,6 +448,7 @@
             ],
             in_specs=[vmem, vmem, vmem],
             out_specs=[vmem, vmem],
+            scratch_shapes=[pltpu.VMEM((6 * k, cols), BF16)],
             compiler_params=pltpu.CompilerParams(vmem_limit_bytes=32 * 2**20),
             name="final",
         )(whitened, gram, factor)

time: 60.2 us -> 58.5 us (0.972)
  local copies, waits for them, and re-layouts: 1.03 us -> 0 us
    unnamed x2 -> x0, local copies, waits for them, and re-layouts: 1.03 us -> none
    pallas_call x1, Pallas kernels: 6.1 us -> 5.22 us  [on_device(): pl.pallas_call(functools.partial(final_kernel, row_factor), out_shape=[ja...]
where the time goes in v3:
time: 58.5 us; the launch traced here: 58.4 us
  Pallas kernels  57.8 us (99%)
  between operations  0.64 us (1%)
    pallas_call x1, Pallas kernels, on_device(): pl.pallas_call(reduce_kernel, out_shape=[jax.ShapeDtypeStruct((k, cols),...  52.5 us
    pallas_call x1, Pallas kernels, on_device(): pl.pallas_call(functools.partial(final_kernel, row_factor), out_shape=[ja...  5.22 us

profile of v3, /device:TPU:1, one launch (start us, length us, event | category | flops | bytes accessed | tf_op | source)
XLA Modules:
  0.0 58.4 jit_solution(5969682229212780668)
XLA Ops:
  0.6 52.5 %image_and_sum.1 = (f32[128,2048]{1,0:T(8,128)S(1)}, f32[128,128]{1,0:T(8,128)S(1)}, f32[128,128]{1,0:T(8,128)S(1)}) custom-call(bf16[5120,2048]{1,0:T(8,128)(2,1)} %a_hbm.1, bf16[2048,128]{1,0:T(8,128)(2,1)} %q_hbm.1), custom_call_target="tpu_custom_call" | custom-call | tf_op jit(solution)/shard_map/image_and_sum/pallas_call | solution.py:406
  53.2 5.2 %final.1 = (f32[2048,128]{1,0:T(8,128)}, f32[128,128]{1,0:T(8,128)}) custom-call(f32[128,2048]{1,0:T(8,128)S(1)} %get-tuple-element.5.s_ref, f32[128,128]{1,0:T(8,128)S(1)} %get-tuple-element.6.gram_ref, f32[128,128]{1,0:T(8,128)S(1)} %get-tuple-element.7.factor_ref), custom_call_target="tpu_custom_call" | custom-call | tf_op jit(solution)/shard_map/final/pallas_call | solution.py:443

commit v4 on v3

--- a/solution.py
+++ b/solution.py
@@ -15,7 +15,12 @@
 LAG = 3
 FLIGHT = 3
 WIDTH, STEP = 32, 8
-ORDER = (("T", 1), ("T", 2), ("T", 3), ("G", 0), ("A", 0), ("A", 1), ("A", 2), ("G", 1), ("A", 3), ("B", 0), ("B", 1), ("G", 2), ("B", 2), ("H", 0), ("B", 3), ("E", 0), ("C", 0), ("C", 1), ("E", 1), ("C", 2), ("E", 2), ("C", 3), ("E", 3), ("W", 0), ("D", 0), ("S", 0), ("D", 1), ("S", 1), ("D", 2), ("S", 2), ("D", 3), ("S", 3), )
+ORDER = (
+    ("T", 1), ("T", 2), ("T", 3), ("A", 0), ("G", 0), ("A", 1), ("A", 2), ("A", 3), ("G", 1), ("B", 0),
+    ("B", 1), ("B", 2), ("G", 2), ("B", 3), ("H", 0), ("E", 0), ("C", 0), ("C", 1), ("E", 1), ("C", 2),
+    ("E", 2), ("C", 3), ("E", 3), ("W", 0), ("D", 0), ("S", 0), ("D", 1), ("S", 1), ("D", 2), ("S", 2),
+    ("D", 3), ("S", 3),
+)
 
 
 STRIDES = (1, 4, 16)

time: 58.5 us -> 58 us (level)
  no operation moved by 1% of the time
where the time goes in v4:
time: 58 us; the launch traced here: 57.9 us
  Pallas kernels  57.3 us (99%)
  between operations  0.64 us (1%)
    pallas_call x1, Pallas kernels, on_device(): pl.pallas_call(reduce_kernel, out_shape=[jax.ShapeDtypeStruct((k, cols),...  52.1 us
    pallas_call x1, Pallas kernels, on_device(): pl.pallas_call(functools.partial(final_kernel, row_factor), out_shape=[ja...  5.22 us

profile of v4, /device:TPU:1, one launch (start us, length us, event | category | flops | bytes accessed | tf_op | source)
XLA Modules:
  0.0 57.9 jit_solution(3357209396446214613)
XLA Ops:
  0.6 52.1 %image_and_sum.1 = (f32[128,2048]{1,0:T(8,128)S(1)}, f32[128,128]{1,0:T(8,128)S(1)}, f32[128,128]{1,0:T(8,128)S(1)}) custom-call(bf16[5120,2048]{1,0:T(8,128)(2,1)} %a_hbm.1, bf16[2048,128]{1,0:T(8,128)(2,1)} %q_hbm.1), custom_call_target="tpu_custom_call" | custom-call | tf_op jit(solution)/shard_map/image_and_sum/pallas_call | solution.py:411
  52.7 5.2 %final.1 = (f32[2048,128]{1,0:T(8,128)}, f32[128,128]{1,0:T(8,128)}) custom-call(f32[128,2048]{1,0:T(8,128)S(1)} %get-tuple-element.5.s_ref, f32[128,128]{1,0:T(8,128)S(1)} %get-tuple-element.6.gram_ref, f32[128,128]{1,0:T(8,128)S(1)} %get-tuple-element.7.factor_ref), custom_call_target="tpu_custom_call" | custom-call | tf_op jit(solution)/shard_map/final/pallas_call | solution.py:448
